TPU v7x, 32 devices: a whole 2x2x4 slice. The times are simulated.
32 devices in a mesh: grp: 2 (over x), wid: 4 (over y, core), hid: 4 (over z).
Axes of the slice: x: 2, y: 2, z: 4, core: 2. Of those that a mesh axis runs over, the one named last changes fastest.
Arguments:
- tokens: bfloat16 [1536, 6144], P(('grp', 'hid'), 'wid'), parts along dimension 0, may hold values from -6 to 6
- expert_ids: int32 [1536, 2], P('grp'), parts along dimension 0, may hold values from 0 to 3, all different within a row
- gate_probs: float32 [1536, 2], P('grp'), parts along dimension 0, may hold values from 0.1 to 0.9
- gate_weight: bfloat16 [4, 6144, 8192], P(None, 'wid', 'hid'), may hold values from -0.078125 to 0.078125
- up_weight: bfloat16 [4, 6144, 8192], P(None, 'wid', 'hid'), may hold values from -0.078125 to 0.078125
- down_weight: bfloat16 [4, 8192, 6144], P(None, 'hid', 'wid'), may hold values from -0.0625 to 0.0625
Outputs:
- mixed: bfloat16 [1536, 6144], P(('grp', 'hid'), 'wid'), parts along dimension 0
There are 2 independent parts, one for each index of `grp`. A program takes and returns all parts, laid end to end along the dimension named above; an argument that names none is the same for every part. Nothing has to cross between parts.
Inputs may be any that keep to these rules, and one draw needn't show every extreme that they name: `expert_ids`: each row names 2 different experts; every expert is named by some row.
All inputs are finite; a program needn't handle non-finite values.
Results may differ from a plain program's by a relative error of at most 0.02.
Values may be sent and summed in bfloat16 or wider, within the bound.
A program may use at most 256 MiB of HBM per device.

v0:
```python
import jax
import jax.numpy as jnp
from jax import lax
from jax.sharding import PartitionSpec as P


def shards(tokens, expert_ids, gate_probs, gate_weight, up_weight, down_weight):
    rows_all = lax.all_gather(tokens, "hid", axis=0, tiled=True)
    row_count = expert_ids.shape[0]
    top_count = expert_ids.shape[1]
    experts = gate_weight.shape[0]
    pair_count = row_count * top_count
    flat_ids = expert_ids.reshape(-1)
    sort_order = jnp.argsort(flat_ids, stable=True)
    counts = jnp.sum(
        (flat_ids[:, None] == jnp.arange(experts, dtype=jnp.int32)[None, :]).astype(jnp.int32),
        axis=0,
    )
    sorted_rows = jnp.take(rows_all, sort_order // top_count, axis=0)
    gate_part = lax.ragged_dot(sorted_rows, gate_weight, counts, preferred_element_type=jnp.float32)
    up_part = lax.ragged_dot(sorted_rows, up_weight, counts, preferred_element_type=jnp.float32)
    gate_sum, up_sum = (
        lax.psum(gate_part.astype(jnp.bfloat16), "wid").astype(jnp.float32),
        lax.psum(up_part.astype(jnp.bfloat16), "wid").astype(jnp.float32),
    )
    hidden = (jax.nn.silu(gate_sum) * up_sum).astype(jnp.bfloat16)
    down_part = lax.ragged_dot(hidden, down_weight, counts, preferred_element_type=jnp.float32)
    inverse = (
        jnp.zeros((pair_count,), jnp.int32)
        .at[sort_order]
        .set(jnp.arange(pair_count, dtype=jnp.int32))
    )
    unsorted = jnp.take(down_part, inverse, axis=0).reshape(
        row_count, top_count, down_part.shape[1]
    )
    combined = jnp.sum(unsorted * gate_probs[:, :, None], axis=1)
    result = lax.psum_scatter(combined.astype(jnp.bfloat16), "hid", scatter_dimension=0, tiled=True)
    return result


def solution(mesh):
    in_specs = (
        P(("grp", "hid"), "wid"),
        P("grp", None),
        P("grp", None),
        P(None, "wid", "hid"),
        P(None, "wid", "hid"),
        P(None, "hid", "wid"),
    )
    out_specs = P(("grp", "hid"), "wid")
    return jax.shard_map(shards, mesh=mesh, in_specs=in_specs, out_specs=out_specs, check_vma=False)
```

profile of v0, /device:TPU:0, one launch (start us, length us, event | category | flops | bytes accessed | tf_op | source)
XLA Modules:
  0.0 510.9 jit_solution(13805130068323542960)
XLA Ops:
  6.5 0.7 all-gather.2.cloned.1.call-update
  7.3 0.9 copy.10
  8.2 0.2 reshape.22
  8.4 5.0 sort.17
  13.5 0.6 convert_reduce_fusion
  14.1 1.4 ragged-dot-metadata
  15.5 46.7 %all-gather.2.cloned.1.call-done = bf16[768,1536]{1,0:T(8,128)(2,1)} async-done(((bf16[192,1536]{1,0:T(8,128)(2,1)}), bf16[768,1536]{1,0:T(8,128)(2,1)}) %all-gather.2.cloned.1.call-update) | async-done | bytes 2359312 | tf_op jit(solution)/shard_map/all_gather | solution.py:8
  62.2 12.4 %gather_fusion = bf16[1536,1536]{1,0:T(8,128)(2,1)} fusion(bf16[768,1536]{1,0:T(8,128)(2,1)} %all-gather.2.cloned.1.call-done, s32[2048]{0:T(1024)S(1)} %pad_clamp_fusion.1), kind=kCustom, calls=%fused_computation | custom fusion | bytes 9443328 | tf_op jit(solution)/shard_map/jit(_take)/gather | solution.py:19
  74.5 5.0 broadcast_select_fusion
  79.5 27.7 %ragged-dot-none.2 = f32[1536,2048]{1,0:T(8,128)} custom-call(s32[1]{0:T(128)} %get-tuple-element.7, s32[5]{0:T(128)} %get-tuple-element.8, s32[9]{0:T(128)} %get-tuple-element.9, s32[9]{0:T(128)} %get-tuple-element.10, s32[1]{0:T(128)} %get-tuple-element.7, bf16[1536,1536]{1,0:T(8,128)(2,1)} %broadcast_select_fusion, bf16[4,1536,2048]{2,1,0:T(8,128)(2,1)} %param.9), custom_call_target="tpu_custom_call" | custom-call | flops 9663676416 | bytes 42467344 | tf_op jit(solution)/shard_map/ragged_dot_general/ragged-dot-none
  107.2 8.2 %convert_element_type.22 = bf16[1536,2048]{1,0:T(8,128)(2,1)} convert(f32[1536,2048]{1,0:T(8,128)} %ragged-dot-none.2) | non-fusion elementwise | flops 3145728 | bytes 18874368 | tf_op jit(solution)/shard_map/convert_element_type | solution.py:23
  115.4 27.7 %ragged-dot-none.1 = f32[1536,2048]{1,0:T(8,128)} custom-call(s32[1]{0:T(128)} %get-tuple-element.7, s32[5]{0:T(128)} %get-tuple-element.8, s32[9]{0:T(128)} %get-tuple-element.9, s32[9]{0:T(128)} %get-tuple-element.10, s32[1]{0:T(128)} %get-tuple-element.7, bf16[1536,1536]{1,0:T(8,128)(2,1)} %broadcast_select_fusion, bf16[4,1536,2048]{2,1,0:T(8,128)(2,1)} %param.10), custom_call_target="tpu_custom_call" | custom-call | flops 9663676416 | bytes 42467344 | tf_op jit(solution)/shard_map/ragged_dot_general/ragged-dot-none
  143.1 8.3 %convert_element_type.24 = bf16[1536,2048]{1,0:T(8,128)(2,1)} convert(f32[1536,2048]{1,0:T(8,128)} %ragged-dot-none.1) | non-fusion elementwise | flops 3145728 | bytes 18874368 | tf_op jit(solution)/shard_map/convert_element_type | solution.py:24
  151.4 0.0 reduce-scatter.2.cloned.1.call-start
  151.5 6.2 %scatter_custom_fusion = s32[1536]{0:T(1024)S(1)} fusion(s32[1536]{0:T(1024)S(1)} %add_select_fusion.1, s32[1536]{0:T(1024)S(1)} %iota.12, s32[]{:T(128)} %constant.41.clone.1), kind=kCustom, calls=%fused_computation.28 | custom fusion | bytes 6148 | tf_op jit(solution)/shard_map/scatter | solution.py:31
  157.7 0.4 broadcast_in_dim.32
  158.1 0.2 copy.11
  158.3 213.1 %all-reduce.3.cloned.1.call-done = (bf16[1536,2048]{1,0:T(8,128)(2,1)}, bf16[1536,2048]{1,0:T(8,128)(2,1)}) async-done(((bf16[1536,2048]{1,0:T(8,128)(2,1)}, bf16[1536,2048]{1,0:T(8,128)(2,1)}), (bf16[1536,2048]{1,0:T(8,128)(2,1)}, bf16[1536,2048]{1,0:T(8,128)(2,1)})) %all-reduce.3.cloned.1.call-update) | async-done | bytes 12582928 | tf_op jit(solution)/shard_map/psum | solution.py:24
  371.4 10.1 %fusion.4 = bf16[1536,2048]{1,0:T(8,128)(2,1)} fusion(bf16[1536,2048]{1,0:T(8,128)(2,1)} %get-tuple-element.19, bf16[1536,2048]{1,0:T(8,128)(2,1)} %get-tuple-element.20), kind=kLoop, calls=%fused_computation.9 | loop fusion | flops 25165824 | bytes 18874368 | tf_op jit(solution)/shard_map/convert_element_type | solution.py:26
  381.5 27.3 %ragged-dot-none = f32[1536,1536]{1,0:T(8,128)} custom-call(s32[1]{0:T(128)} %get-tuple-element.7, s32[5]{0:T(128)} %get-tuple-element.8, s32[9]{0:T(128)} %get-tuple-element.9, s32[9]{0:T(128)} %get-tuple-element.10, s32[1]{0:T(128)} %get-tuple-element.7, bf16[1536,2048]{1,0:T(8,128)(2,1)} %fusion.4, bf16[4,2048,1536]{2,1,0:T(8,128)(2,1)} %param.11), custom_call_target="tpu_custom_call" | custom-call | flops 9663676416 | bytes 40894480 | tf_op jit(solution)/shard_map/ragged_dot_general/ragged-dot-none
  408.8 14.1 %gather_fusion.1 = f32[1536,1536]{1,0:T(8,128)} fusion(f32[1536,1536]{1,0:T(8,128)} %ragged-dot-none, s32[2048]{0:T(1024)S(1)} %pad_clamp_fusion), kind=kCustom, calls=%fused_computation.1 | custom fusion | bytes 18880512 | tf_op jit(solution)/shard_map/jit(_take)/gather | solution.py:33
  422.9 11.9 %gather.12 = f32[768,2,1536]{2,1,0:T(2,128)} reshape(f32[1536,1536]{1,0:T(8,128)} %gather_fusion.1) | data formatting | bytes 18874368 | tf_op jit(solution)/shard_map/jit(_take)/gather | solution.py:33
  434.8 21.2 %multiply_reduce_fusion = bf16[768,1536]{1,0:T(8,128)(2,1)} fusion(f32[768,2,1536]{2,1,0:T(2,128)} %gather.12, pred[768,2]{1,0:T(8,128)(4,1)S(1)} %broadcast_in_dim.32, f32[768,2]{1,0:T(8,128)S(1)} %copy.11), kind=kLoop, calls=%fused_computation.10 | loop fusion | flops 5898240 | bytes 11804160 | tf_op jit(solution)/shard_map/reduce_sum | solution.py:36
  456.0 48.4 %reduce-scatter.2.cloned.1.call-done = bf16[192,1536]{1,0:T(8,128)(2,1)} async-done(((bf16[768,1536]{1,0:T(8,128)(2,1)}), bf16[192,1536]{1,0:T(8,128)(2,1)}) %reduce-scatter.2.cloned.1.call-update) | async-done | bytes 589840 | tf_op jit(solution)/shard_map/reduce_scatter | solution.py:37
  (14 shorter events, 0.1 us)
Async XLA Ops:
  6.5 55.6 %all-gather.2.cloned.1.call-start = ((), (), s32[]{:S(2)}) async-start(), calls=%async_computation.1 | async-start | bytes 2949120 | tf_op jit(solution)/shard_map/all_gather | solution.py:8
  7.3 364.2 %all-reduce.3.cloned.1.call-start = ((), (), s32[]{:S(2)}) async-start(), calls=%async_computation.3 | async-start | bytes 25165824 | tf_op jit(solution)/shard_map/psum | solution.py:24
  151.4 6.7 %copy-start = (f32[768,2]{0,1:T(2,128)S(1)}, f32[768,2]{0,1:T(2,128)}, u32[]{:S(2)}) copy-start(f32[768,2]{0,1:T(2,128)} %param.8) | copy-start | bytes 18436
  151.4 353.0 %reduce-scatter.2.cloned.1.call-start = ((), (), s32[]{:S(2)}) async-start(), calls=%async_computation.2 | async-start | bytes 2949120 | tf_op jit(solution)/shard_map/reduce_scatter | solution.py:37
Sparse Core Ops, SparseCore 0:
  8.9 53.2 all-gather.1
  151.5 219.8 all-reduce.2
  456.1 48.2 reduce-scatter.1
where the time goes:
time: 512 us; the launch traced here: 511 us
  waiting for transfers between devices  309 us (60%)
  Pallas kernels  84.1 us (16%)
  other arithmetic  58.5 us (11%)
  local copies, waits for them, and re-layouts  46.2 us (9%)
  between operations  13.2 us (3%)
    psum x1, waiting for transfers between devices, shards(): lax.psum(up_part.astype(jnp.bfloat16), 'wid').astype(jnp.float32)  213 us
    another operation x3, Pallas kernels  82.7 us
    reduce_scatter x1, waiting for transfers between devices, shards(): lax.psum_scatter(combined.astype(jnp.bfloat16), 'hid', scatter_dimension=...  48.4 us
    all_gather x1, waiting for transfers between devices, shards(): rows_all = lax.all_gather(tokens, 'hid', axis=0, tiled=True)  46.7 us
    gather x2, local copies, waits for them, and re-layouts, shards(): jnp.take(down_part, inverse, axis=0)  26 us
    reduce_sum x1, other arithmetic, shards(): combined = jnp.sum(unsorted * gate_probs[:, :, None], axis=1)  21.2 us
    gather x1, local copies, waits for them, and re-layouts, shards(): sorted_rows = jnp.take(rows_all, sort_order // top_count, axis=0)  12.4 us
  transfers between devices with their start and end apart: 3, of which 3 were waited for; matrix products, arithmetic and copies ran while one was open for 3% of the time, Pallas kernels for 0%

commit v1 on v0

v1 whole, which is shorter than its diff:
```python
import functools

import jax
import jax.numpy as jnp
from jax import lax
from jax.experimental import pallas as pl
from jax.experimental.pallas import tpu as pltpu
from jax.sharding import PartitionSpec as P

MESH = pl.DeviceIdType.MESH
TOP = 2
H_SLOTS = 4


def block_at(me, apart, count):
    if count & (count - 1):
        return lax.rem(me + apart, count)
    total, bit = 0, 1
    while bit < count:
        total = total + bit * (((me // bit) % 2 + (apart // bit) % 2) % 2)
        bit *= 2
    return total


def back_at(apart, count):
    return apart if count & (count - 1) == 0 else count - apart


def kernel(
    n_wid, n_hid, width,
    tok_ref, ids_ref, probs_ref, gate_hbm, up_hbm, down_hbm, out_ref,
    x_all, w_gate, w_up, w_down, pre, s1_send, s1_recv, mine, s2_send, s2_recv, hidden, spread, acc, out_send, out_recv,
    w_sem, d_sem, x_ssem, x_rsem, s1_ssem, s1_rsem, s2_ssem, s2_rsem, s3_ssem, s3_rsem, s4_ssem, s4_rsem, o_ssem, o_rsem,
):
    rows, depth = tok_ref.shape
    experts, units = gate_hbm.shape[0], gate_hbm.shape[2]
    half = width // 2
    cuts = units // width
    steps = n_hid * cuts
    early = max(cuts - 1, 1)
    pairs = TOP * rows
    n_y = n_wid // 2
    share = pairs // n_y
    tile = 512 if depth % 512 == 0 else depth

    wid = lax.axis_index("wid")
    hid = lax.axis_index("hid")
    core = wid % 2
    y = wid // 2
    other = y * 2 + (1 - core)

    def y_at(shift):
        return (y + shift) % n_y

    def place(step):
        rest = step - early
        later = n_hid - 1 - rest // cuts
        is_first = step < early
        is_last = step >= early + (n_hid - 1) * cuts
        apart = jnp.where(is_first | is_last, 0, later)
        cut = jnp.where(is_first, step, jnp.where(is_last, step - (steps - cuts), rest % cuts))
        return apart, cut

    def first_use(apart):
        return early + (n_hid - 1 - apart) * cuts

    def weights_copy(step, slot):
        columns = pl.ds(pl.multiple_of(place(step)[1] * width, width), width)
        return [
            pltpu.make_async_copy(gate_hbm.at[:, :, columns], w_gate.at[slot], w_sem.at[slot, 0]),
            pltpu.make_async_copy(up_hbm.at[:, :, columns], w_up.at[slot], w_sem.at[slot, 1]),
        ]

    def down_copy(step, slot):
        lines = pl.ds(pl.multiple_of(place(step)[1] * width, width), width)
        return [
            pltpu.make_async_copy(
                down_hbm.at[e, lines, :], w_down.at[slot, pl.ds(e * width, width), :], d_sem.at[slot, e]
            )
            for e in range(experts)
        ]

    def start_all(copies):
        for copy in copies:
            copy.start()

    def token_copy(apart):
        return pltpu.make_async_remote_copy(
            src_ref=tok_ref, dst_ref=x_all.at[back_at(apart, n_hid)],
            send_sem=x_ssem.at[apart - 1], recv_sem=x_rsem.at[back_at(apart, n_hid) - 1],
            device_id={"hid": block_at(hid, apart, n_hid)}, device_id_type=MESH,
        )

    def token_arrival(apart):
        return pltpu.make_async_remote_copy(
            src_ref=tok_ref, dst_ref=x_all.at[apart],
            send_sem=x_ssem.at[apart - 1], recv_sem=x_rsem.at[apart - 1],
            device_id={"hid": block_at(hid, apart, n_hid)}, device_id_type=MESH,
        )

    def out_copy(apart, landing):
        return pltpu.make_async_remote_copy(
            src_ref=out_send.at[apart - 1], dst_ref=out_recv.at[landing - 1],
            send_sem=o_ssem.at[apart - 1], recv_sem=o_rsem.at[landing - 1],
            device_id={"hid": block_at(hid, apart, n_hid)}, device_id_type=MESH,
        )

    def s1_copy(step):
        slot = step % 2
        return pltpu.make_async_remote_copy(
            src_ref=s1_send, dst_ref=s1_recv.at[slot], send_sem=s1_ssem, recv_sem=s1_rsem.at[slot],
            device_id={"wid": other}, device_id_type=MESH,
        )

    def s2_copy(step, shift):
        slot, to = step % 2, y_at(shift)
        return pltpu.make_async_remote_copy(
            src_ref=s2_send.at[:, pl.ds(pl.multiple_of(to * share, share), share), :],
            dst_ref=s2_recv.at[slot, shift - 1],
            send_sem=s2_ssem.at[shift - 1], recv_sem=s2_rsem.at[slot, shift - 1],
            device_id={"wid": to * 2 + core}, device_id_type=MESH,
        )

    def s3_copy(step, shift, owner):
        slot = step % H_SLOTS
        part = hidden.at[slot, core, pl.ds(pl.multiple_of(owner * share, share), share), :]
        return pltpu.make_async_remote_copy(
            src_ref=part, dst_ref=part,
            send_sem=s3_ssem.at[shift - 1], recv_sem=s3_rsem.at[slot, shift - 1],
            device_id={"wid": y_at(shift) * 2 + core}, device_id_type=MESH,
        )

    def s4_copy(step, which):
        slot = step % H_SLOTS
        part = hidden.at[slot, which]
        return pltpu.make_async_remote_copy(
            src_ref=part, dst_ref=part, send_sem=s4_ssem.at[step % 2], recv_sem=s4_rsem.at[slot],
            device_id={"wid": other}, device_id_type=MESH,
        )

    start_all(weights_copy(0, 0))
    barrier = pltpu.get_barrier_semaphore()
    pl.semaphore_signal(barrier, inc=1, device_id={"wid": other}, device_id_type=MESH)
    for shift in range(1, n_y):
        pl.semaphore_signal(barrier, inc=1, device_id={"wid": y_at(shift) * 2 + core}, device_id_type=MESH)
    for apart in range(1, n_hid):
        pl.semaphore_signal(barrier, inc=1, device_id={"hid": block_at(hid, apart, n_hid)}, device_id_type=MESH)
    pl.semaphore_wait(barrier, n_y + n_hid - 1)

    token_copy(n_hid - 1).start()
    x_all[0] = tok_ref[...]
    start_all(down_copy(0, 0))

    def stage_d(step):
        for shift in range(1, n_y):
            s3_copy(step, shift, y).wait_send()
            s3_copy(step, shift, y_at(n_y - shift)).wait_recv()
        s4_copy(step, core).start()

    def stage_c(step):
        slot = step % 2
        gate, up = mine[0], mine[1]
        for shift in range(1, n_y):
            s2_copy(step, shift).wait_send()
            s2_copy(step, shift).wait_recv()
        for shift in range(1, n_y):
            gate = gate + s2_recv[slot, shift - 1, 0].astype(jnp.float32)
            up = up + s2_recv[slot, shift - 1, 1].astype(jnp.float32)
        block = block_at(hid, place(step)[0], n_hid)
        factor = probs_ref[pl.ds(pl.multiple_of(block * pairs + y * share, share), share), :]
        value = gate / (1.0 + jnp.exp(-gate)) * up * factor
        hidden[step % H_SLOTS, core, pl.ds(pl.multiple_of(y * share, share), share), :] = value.astype(jnp.bfloat16)
        for shift in range(1, n_y):
            s3_copy(step, shift, y).start()

    def stage_b(step):
        slot = step % 2
        s1_copy(step).wait_send()
        s1_copy(step).wait_recv()
        columns = pl.ds(pl.multiple_of(core * half, half), half)
        own = pl.ds(pl.multiple_of(y * share, share), share)
        for which in range(2):
            s2_send[which] = (pre[which, :, columns] + s1_recv[slot, which].astype(jnp.float32)).astype(jnp.bfloat16)
            mine[which] = pre[which, own, columns] + s1_recv[slot, which, own, :].astype(jnp.float32)
        for shift in range(1, n_y):
            s2_copy(step, shift).start()

    def stage_a(step):
        slot = step % 2
        for copy in weights_copy(step, slot):
            copy.wait()
        apart, cut = place(step)
        block = block_at(hid, apart, n_hid)
        x = x_all[apart]
        base = pl.multiple_of(block * pairs, pairs)
        ids = [ids_ref[pl.ds(pl.multiple_of(base + k * rows, rows), rows), :] for k in range(TOP)]
        for which, weight in ((0, w_gate), (1, w_up)):
            for e in range(experts):
                value = jnp.dot(x, weight[slot, e], preferred_element_type=jnp.float32)
                for k in range(TOP):
                    lines = slice(k * rows, (k + 1) * rows)
                    if e == 0:
                        pre[which, lines, :] = value
                    else:
                        pre[which, lines, :] = jnp.where(ids[k] == e, value, pre[which, lines, :])
        columns = pl.ds(pl.multiple_of((1 - core) * half, half), half)
        for which in range(2):
            s1_send[which] = pre[which, :, columns].astype(jnp.bfloat16)
        s1_copy(step).start()

    def stage_e(step):
        slot = step % 2
        s4_copy(step, core).wait_send()
        s4_copy(step, 1 - core).wait_recv()

        @pl.when(step + 1 < steps)
        def _():
            start_all(down_copy(step + 1, (step + 1) % 2))

        apart, cut = place(step)
        block = block_at(hid, apart, n_hid)
        base = pl.multiple_of(block * pairs, pairs)
        ids = [ids_ref[pl.ds(pl.multiple_of(base + k * rows, rows), rows), :] for k in range(TOP)]
        for side in range(2):
            parts = [hidden[step % H_SLOTS, side, k * rows:(k + 1) * rows, :].astype(jnp.float32) for k in range(TOP)]
            for e in range(experts):
                chosen = jnp.where(ids[0] == e, parts[0], jnp.where(ids[1] == e, parts[1], 0.0))
                start = e * width + side * half
                spread[:, start:start + half] = chosen.astype(jnp.bfloat16)
        for copy in down_copy(step, slot):
            copy.wait()
        keep = jnp.where(apart == 0, 0, 1)

        @pl.when((step == 0) | ((apart > 0) & (cut == 0)))
        def _():
            acc[keep] = jnp.zeros(acc.shape[1:], jnp.float32)

        for start in range(0, depth, tile):
            acc[keep, :, start:start + tile] += jnp.dot(
                spread[...], w_down[slot, :, start:start + tile], preferred_element_type=jnp.float32
            )

        for far in range(1, n_hid):
            @pl.when((apart == far) & (cut == cuts - 1))
            def _():
                out_send[far - 1] = acc[1].astype(jnp.bfloat16)
                out_copy(far, back_at(far, n_hid)).start()

    def body(i, carry):
        def at(step, stage):
            @pl.when((step >= 0) & (step < steps))
            def _():
                stage(step)

        @pl.when(i + 1 < steps)
        def _():
            start_all(weights_copy(i + 1, (i + 1) % 2))

        for apart in range(1, n_hid):
            if apart < n_hid - 1:
                @pl.when(i == first_use(apart + 1) - 1)
                def _():
                    token_copy(apart).start()

            @pl.when(i == first_use(apart))
            def _():
                token_arrival(apart).wait_recv()

        at(i - 3, stage_d)
        at(i - 2, stage_c)
        at(i - 1, stage_b)
        at(i, stage_a)
        at(i - 4, stage_e)
        return carry

    lax.fori_loop(0, steps + 4, body, 0)

    total = acc[0]
    for apart in range(1, n_hid):
        token_copy(apart).wait_send()
        out_copy(apart, apart).wait_send()
        out_copy(apart, apart).wait_recv()
        total = total + out_recv[apart - 1].astype(jnp.float32)
    out_ref[...] = total.astype(jnp.bfloat16)


def shards(n_wid, n_hid, tokens, expert_ids, gate_probs, gate_weight, up_weight, down_weight):
    rows, depth = tokens.shape
    experts, _, units = gate_weight.shape
    width = 512
    half = width // 2
    n_y = n_wid // 2
    pairs = TOP * rows
    share = pairs // n_y
    ids = expert_ids.reshape(n_hid, rows, TOP).transpose(0, 2, 1).reshape(n_hid * pairs, 1)
    probs = gate_probs.reshape(n_hid, rows, TOP).transpose(0, 2, 1).reshape(n_hid * pairs, 1)
    vmem = pl.BlockSpec(memory_space=pltpu.VMEM)
    hbm = pl.BlockSpec(memory_space=pl.ANY)
    bf16, f32 = jnp.bfloat16, jnp.float32
    dma = pltpu.SemaphoreType.DMA
    work = 2 * n_hid * rows * experts * depth * units * 3
    return pl.pallas_call(
        functools.partial(kernel, n_wid, n_hid, width),
        out_shape=jax.ShapeDtypeStruct((rows, depth), bf16),
        in_specs=[vmem, vmem, vmem, hbm, hbm, hbm],
        out_specs=vmem,
        scratch_shapes=[
            pltpu.VMEM((n_hid, rows, depth), bf16),
            pltpu.VMEM((2, experts, depth, width), bf16),
            pltpu.VMEM((2, experts, depth, width), bf16),
            pltpu.VMEM((2, experts * width, depth), bf16),
            pltpu.VMEM((2, pairs, width), f32),
            pltpu.VMEM((2, pairs, half), bf16),
            pltpu.VMEM((2, 2, pairs, half), bf16),
            pltpu.VMEM((2, share, half), f32),
            pltpu.VMEM((2, pairs, half), bf16),
            pltpu.VMEM((2, n_y - 1, 2, share, half), bf16),
            pltpu.VMEM((H_SLOTS, 2, pairs, half), bf16),
            pltpu.VMEM((rows, experts * width), bf16),
            pltpu.VMEM((2, rows, depth), f32),
            pltpu.VMEM((n_hid - 1, rows, depth), bf16),
            pltpu.VMEM((n_hid - 1, rows, depth), bf16),
            dma((2, 2)),
            dma((2, experts)),
            dma((n_hid - 1,)),
            dma((n_hid - 1,)),
            dma,
            dma((2,)),
            dma((n_y - 1,)),
            dma((2, n_y - 1)),
            dma((n_y - 1,)),
            dma((H_SLOTS, n_y - 1)),
            dma((2,)),
            dma((H_SLOTS,)),
            dma((n_hid - 1,)),
            dma((n_hid - 1,)),
        ],
        compiler_params=pltpu.CompilerParams(
            collective_id=0, has_side_effects=True, vmem_limit_bytes=60 * 1024 * 1024
        ),
        cost_estimate=pl.CostEstimate(
            flops=work, bytes_accessed=n_hid * experts * depth * units * 6, transcendentals=0
        ),
        name="expert_layer",
    )(tokens, ids, probs, gate_weight, up_weight, down_weight)


def solution(mesh):
    in_specs = (
        P(("grp", "hid"), "wid"),
        P("grp", None),
        P("grp", None),
        P(None, "wid", "hid"),
        P(None, "wid", "hid"),
        P(None, "hid", "wid"),
    )
    out_specs = P(("grp", "hid"), "wid")
    return jax.shard_map(
        functools.partial(shards, mesh.shape["wid"], mesh.shape["hid"]),
        mesh=mesh, in_specs=in_specs, out_specs=out_specs, check_vma=False,
    )
```

time: 512 us -> 165 us (0.32)
  waiting for transfers between devices: 309 us -> 0 us
  Pallas kernels: 84.1 us -> 158 us
  other arithmetic: 58.5 us -> 0 us
  local copies, waits for them, and re-layouts: 46.2 us -> 6.6 us
  between operations: 13.2 us -> 0.01 us
    psum x1 -> x0, waiting for transfers between devices: 213 us -> none  [shards(): lax.psum(up_part.astype(jnp.bfloat16), 'wid').astype(jnp.float32)]
    pallas_call x0 -> x1, Pallas kernels: none -> 158 us  [shards(): pl.pallas_call(functools.partial(kernel, n_wid, n_hid, width), out_shape=...]
    another operation x3 -> x0, Pallas kernels: 82.7 us -> none
    reduce_scatter x1 -> x0, waiting for transfers between devices: 48.4 us -> none  [shards(): lax.psum_scatter(combined.astype(jnp.bfloat16), 'hid', scatter_dimension=...]
    all_gather x1 -> x0, waiting for transfers between devices: 46.7 us -> none  [shards(): rows_all = lax.all_gather(tokens, 'hid', axis=0, tiled=True)]
    gather x3 -> x0, local copies, waits for them, and re-layouts: 38.4 us -> none  [the longest x2 26 us: shards(): jnp.take(down_part, inverse, axis=0)]
    convert_element_type x3 -> x0, other arithmetic: 26.6 us -> none  [the longest x1 10.1 us: shards(): hidden = (jax.nn.silu(gate_sum) * up_sum).astype(jnp.bfloat16)]
    reduce_sum x2 -> x0, other arithmetic: 21.8 us -> none  [the longest x1 21.2 us: shards(): combined = jnp.sum(unsorted * gate_probs[:, :, None], axis=1)]
  transfers between devices with their start and end apart: 3 -> 0, of which waited for: 3 -> 0; matrix products, arithmetic and copies ran while one was open for 3% -> 0% of each run, Pallas kernels for 0% -> 0%
where the time goes in v1:
time: 165 us; the launch traced here: 164 us
  Pallas kernels  158 us (96%)
  local copies, waits for them, and re-layouts  6.6 us (4%)
    pallas_call x1, Pallas kernels, shards(): pl.pallas_call(functools.partial(kernel, n_wid, n_hid, width), out_shape=...  158 us

profile of v1, /device:TPU:0, one launch (start us, length us, event | category | flops | bytes accessed | tf_op | source)
XLA Modules:
  0.0 164.4 jit_solution(1779588300089966215)
XLA Ops:
  0.0 0.8 reshape.12
  0.8 0.8 reshape.14
  1.6 1.6 reshape.17.probs_ref
  3.1 1.5 reshape.16.ids_ref
  4.7 157.8 %expert_layer.1 = bf16[192,1536]{1,0:T(8,128)(2,1)} custom-call(bf16[192,1536]{1,0:T(8,128)(2,1)} %tok_ref.1, s32[1536,1]{1,0:T(8,128)} %reshape.16.ids_ref, f32[1536,1]{1,0:T(8,128)} %reshape.17.probs_ref, bf16[4,1536,2048]{2,1,0:T(8,128)(2,1)} %gate_hbm.1, bf16[4,1536,2048]{2,1,0:T(8,128)(2,1)} %up_hbm.1, bf16[4,2048,1536]{2,1,0:T(8,128)(2,1)} %down_hbm.1), custom_call_target="tpu_custom_call" | custom-call | flops 57982058496 | bytes 301989888 | tf_op jit(solution)/shard_map/expert_layer/pallas_call | solution.py:302
  162.5 1.9 %copy.18 = bf16[192,1536]{1,0:T(8,128)(2,1)} copy(bf16[192,1536]{1,0:T(8,128)(2,1)} %expert_layer.1) | data formatting | bytes 1179648
  (2 shorter events, 0.0 us)

commit v2 on v1

--- a/solution.py
+++ b/solution.py
@@ -29,7 +29,7 @@
 def kernel(
     n_wid, n_hid, width,
     tok_ref, ids_ref, probs_ref, gate_hbm, up_hbm, down_hbm, out_ref,
-    x_all, w_gate, w_up, w_down, pre, s1_send, s1_recv, mine, s2_send, s2_recv, hidden, spread, acc, out_send, out_recv,
+    x_all, w_gate, w_up, w_down, pre, s1_send, s1_recv, mine, s2_send, s2_recv, hidden, spread, acc, out_send, out_recv, factors,
     w_sem, d_sem, x_ssem, x_rsem, s1_ssem, s1_rsem, s2_ssem, s2_rsem, s3_ssem, s3_rsem, s4_ssem, s4_rsem, o_ssem, o_rsem,
 ):
     rows, depth = tok_ref.shape
@@ -149,6 +149,10 @@
 
     token_copy(n_hid - 1).start()
     x_all[0] = tok_ref[...]
+    for block in range(n_hid):
+        for k in range(TOP):
+            start = block * pairs + k * rows
+            factors[start:start + rows, :] = probs_ref[block * rows:(block + 1) * rows, k:k + 1]
     start_all(down_copy(0, 0))
 
     def stage_d(step):
@@ -167,7 +171,7 @@
             gate = gate + s2_recv[slot, shift - 1, 0].astype(jnp.float32)
             up = up + s2_recv[slot, shift - 1, 1].astype(jnp.float32)
         block = block_at(hid, place(step)[0], n_hid)
-        factor = probs_ref[pl.ds(pl.multiple_of(block * pairs + y * share, share), share), :]
+        factor = factors[pl.ds(pl.multiple_of(block * pairs + y * share, share), share), :]
         value = gate / (1.0 + jnp.exp(-gate)) * up * factor
         hidden[step % H_SLOTS, core, pl.ds(pl.multiple_of(y * share, share), share), :] = value.astype(jnp.bfloat16)
         for shift in range(1, n_y):
@@ -192,8 +196,8 @@
         apart, cut = place(step)
         block = block_at(hid, apart, n_hid)
         x = x_all[apart]
-        base = pl.multiple_of(block * pairs, pairs)
-        ids = [ids_ref[pl.ds(pl.multiple_of(base + k * rows, rows), rows), :] for k in range(TOP)]
+        lines = pl.ds(pl.multiple_of(block * rows, rows), rows)
+        ids = [ids_ref[lines, k:k + 1] for k in range(TOP)]
         for which, weight in ((0, w_gate), (1, w_up)):
             for e in range(experts):
                 value = jnp.dot(x, weight[slot, e], preferred_element_type=jnp.float32)
@@ -219,8 +223,8 @@
 
         apart, cut = place(step)
         block = block_at(hid, apart, n_hid)
-        base = pl.multiple_of(block * pairs, pairs)
-        ids = [ids_ref[pl.ds(pl.multiple_of(base + k * rows, rows), rows), :] for k in range(TOP)]
+        lines = pl.ds(pl.multiple_of(block * rows, rows), rows)
+        ids = [ids_ref[lines, k:k + 1] for k in range(TOP)]
         for side in range(2):
             parts = [hidden[step % H_SLOTS, side, k * rows:(k + 1) * rows, :].astype(jnp.float32) for k in range(TOP)]
             for e in range(experts):
@@ -292,8 +296,6 @@
     n_y = n_wid // 2
     pairs = TOP * rows
     share = pairs // n_y
-    ids = expert_ids.reshape(n_hid, rows, TOP).transpose(0, 2, 1).reshape(n_hid * pairs, 1)
-    probs = gate_probs.reshape(n_hid, rows, TOP).transpose(0, 2, 1).reshape(n_hid * pairs, 1)
     vmem = pl.BlockSpec(memory_space=pltpu.VMEM)
     hbm = pl.BlockSpec(memory_space=pl.ANY)
     bf16, f32 = jnp.bfloat16, jnp.float32
@@ -320,6 +322,7 @@
             pltpu.VMEM((2, rows, depth), f32),
             pltpu.VMEM((n_hid - 1, rows, depth), bf16),
             pltpu.VMEM((n_hid - 1, rows, depth), bf16),
+            pltpu.VMEM((n_hid * pairs, 1), f32),
             dma((2, 2)),
             dma((2, experts)),
             dma((n_hid - 1,)),
@@ -342,7 +345,7 @@
             flops=work, bytes_accessed=n_hid * experts * depth * units * 6, transcendentals=0
         ),
         name="expert_layer",
-    )(tokens, ids, probs, gate_weight, up_weight, down_weight)
+    )(tokens, expert_ids, gate_probs, gate_weight, up_weight, down_weight)
 
 
 def solution(mesh):

time: 165 us -> 163 us (0.988)
    reshape x6 -> x0, local copies, waits for them, and re-layouts: 4.68 us -> none  [the longest x3 2.36 us: shards(): gate_probs.reshape(n_hid, rows, TOP).transpose(0, 2, 1)]
    unnamed x1 -> x3, local copies, waits for them, and re-layouts: 1.92 us -> 5.17 us
where the time goes in v2:
time: 163 us
  Pallas kernels  158 us (97%)
  local copies, waits for them, and re-layouts  5.17 us (3%)
    pallas_call x1, Pallas kernels, shards(): pl.pallas_call(functools.partial(kernel, n_wid, n_hid, width), out_shape=...  158 us
    unnamed x3, local copies, waits for them, and re-layouts  5.17 us

profile of v2, /device:TPU:0, one launch (start us, length us, event | category | flops | bytes accessed | tf_op | source)
XLA Modules:
  0.0 162.9 jit_solution(13184577589840942685)
XLA Ops:
  0.0 1.6 copy.7.ids_ref
  1.6 1.6 copy.8.probs_ref
  3.3 157.7 %expert_layer.1 = bf16[192,1536]{1,0:T(8,128)(2,1)} custom-call(bf16[192,1536]{1,0:T(8,128)(2,1)} %tok_ref.1, s32[768,2]{1,0:T(8,128)} %copy.7.ids_ref, f32[768,2]{1,0:T(8,128)} %copy.8.probs_ref, bf16[4,1536,2048]{2,1,0:T(8,128)(2,1)} %gate_hbm.1, bf16[4,1536,2048]{2,1,0:T(8,128)(2,1)} %up_hbm.1, bf16[4,2048,1536]{2,1,0:T(8,128)(2,1)} %down_hbm.1), custom_call_target="tpu_custom_call" | custom-call | flops 57982058496 | bytes 301989888 | tf_op jit(solution)/shard_map/expert_layer/pallas_call | solution.py:304
  161.0 1.9 %copy.10 = bf16[192,1536]{1,0:T(8,128)(2,1)} copy(bf16[192,1536]{1,0:T(8,128)(2,1)} %expert_layer.1) | data formatting | bytes 1179648
